TPU v7x, 32 devices: a whole 2x2x4 slice. The times are simulated.
32 devices in a mesh: parts: 2 (over x), row: 16 (over z, y, core).
Axes of the slice: x: 2, y: 2, z: 4, core: 2. Of those that a mesh axis runs over, the one named last changes fastest.
Arguments:
- train_grads: bfloat16 [32768, 4096], P(('parts', 'row')), parts along dimension 0, may hold values from -140 to 140
- query_grads: bfloat16 [256, 4096], P(('parts', 'row')), parts along dimension 0, may hold values from -140 to 140
- inverse_gram: bfloat16 [4096, 4096], P('row'), may hold values from -0.5 to 3.5, as said below
Outputs:
- scores: bfloat16 [32768, 128], P(('parts', 'row')), parts along dimension 0
There are 2 independent parts, one for each index of `parts`. A program takes and returns all parts, laid end to end along the dimension named above; an argument that names none is the same for every part. Nothing has to cross between parts.
Inputs may be any that keep to these rules, and one draw needn't show every extreme that they name: `inverse_gram`: symmetric.
All inputs are finite; a program needn't handle non-finite values.
Results may differ from a plain program's by a relative error of at most 0.0051.
Values may be sent and summed in bfloat16 or wider, within the bound.
A program may use at most 64 MiB of HBM per device.

v0:
```python
import jax
import jax.numpy as jnp
from jax import lax
from jax.sharding import PartitionSpec as P


def inverse_rms(values):
    wide = values.astype(jnp.float32)
    return lax.rsqrt(jnp.mean(wide * wide, axis=1) + 1e-06)


def score_tile(train_grads, train_scale, panel):
    query_scale = inverse_rms(panel)
    raw = lax.dot_general(
        train_grads, panel, (((1,), (1,)), ((), ())), preferred_element_type=jnp.float32
    )
    factor = 1.0 / panel.shape[1] ** 0.5
    return raw * train_scale[:, None] * query_scale[None, :] * factor


def body(train_grads, query_grads, inverse_gram):
    train_scale = inverse_rms(train_grads)
    spread = lax.all_to_all(query_grads, "row", split_axis=1, concat_axis=0, tiled=True)
    owned = lax.psum_scatter(
        jnp.dot(spread, inverse_gram, preferred_element_type=jnp.float32),
        "row",
        scatter_dimension=0,
        tiled=True,
    ).astype(jnp.bfloat16)
    panel = lax.all_gather(owned, "row", axis=0, tiled=True)
    scores = score_tile(train_grads, train_scale, panel)
    return scores.astype(jnp.bfloat16)


def solution(mesh):
    return jax.shard_map(
        body,
        mesh=mesh,
        in_specs=(P(("parts", "row"), None), P(("parts", "row"), None), P("row", None)),
        out_specs=P(("parts", "row"), None),
        check_vma=False,
    )
```

profile of v0, /device:TPU:0, one launch (start us, length us, event | category | flops | bytes accessed | tf_op | source)
XLA Modules:
  0.0 137.1 jit_solution(3694655319736235486)
XLA Ops:
  6.5 0.0 copy-start
  6.5 0.0 reduce-scatter.2.cloned.1.call-start
  6.5 14.4 %all_to_all.19 = bf16[8,16,256]{2,0,1:T(8,128)(2,1)S(1)} all-to-all(bf16[8,16,256]{2,0,1:T(8,128)(2,1)} %bitcast.11), channel_id=1, replica_groups=mesh['parts'=2,'row'=16] {'row'}, dimensions={1} | all-to-all | bytes 131072 | tf_op jit(solution)/shard_map/all_to_all | solution.py:23
  21.0 0.0 copy-done
  21.0 1.8 %fusion.4 = f32[128,4096]{1,0:T(8,128)} fusion(bf16[256,4096]{1,0:T(8,128)(2,1)S(1)} %copy-done, bf16[8,16,256]{2,0,1:T(8,128)(2,1)S(1)} %all_to_all.19), kind=kOutput, calls=%fused_computation.7 | convolution fusion | flops 268435456 | bytes 4259840 | tf_op jit(solution)/shard_map/dot_general | solution.py:25
  22.8 0.0 reduce-scatter.2.cloned.1.call-update
  22.8 0.0 all-gather.2.cloned.1.call-start
  22.8 59.0 %reduce-scatter.2.cloned.1.call-done = f32[8,4096]{1,0:T(8,128)} async-done(((f32[128,4096]{1,0:T(8,128)}), f32[8,4096]{1,0:T(8,128)}) %reduce-scatter.2.cloned.1.call-update) | async-done | bytes 131088 | tf_op jit(solution)/shard_map/reduce_scatter | solution.py:24
  81.8 1.5 %convert_element_type.15 = bf16[8,4096]{1,0:T(8,128)(2,1)} convert(f32[8,4096]{1,0:T(8,128)} %reduce-scatter.2.cloned.1.call-done) | non-fusion elementwise | flops 32768 | bytes 196608 | tf_op jit(solution)/shard_map/convert_element_type | solution.py:29
  83.3 0.0 all-gather.2.cloned.1.call-update
  83.4 5.1 %multiply_reduce_fusion = f32[1024]{0:T(1024)S(1)} fusion(bf16[1024,4096]{1,0:T(8,128)(2,1)} %param.3), kind=kLoop, calls=%fused_computation | loop fusion | flops 12581888 | bytes 8392704 | tf_op jit(solution)/shard_map/reduce_sum | solution.py:9
  88.4 32.8 %all-gather.2.cloned.1.call-done = bf16[128,4096]{1,0:T(8,128)(2,1)} async-done(((bf16[8,4096]{1,0:T(8,128)(2,1)}), bf16[128,4096]{1,0:T(8,128)(2,1)}) %all-gather.2.cloned.1.call-update) | async-done | bytes 1048592 | tf_op jit(solution)/shard_map/all_gather | solution.py:30
  121.2 1.5 %multiply_reduce_fusion.1 = f32[128]{0:T(128)S(1)} fusion(bf16[128,4096]{1,0:T(8,128)(2,1)} %all-gather.2.cloned.1.call-done), kind=kLoop, calls=%fused_computation.1 | loop fusion | flops 1572736 | bytes 1049088 | tf_op jit(solution)/shard_map/reduce_sum | solution.py:9
  122.7 6.6 %fusion.3 = bf16[1024,128]{0,1:T(8,128)(2,1)S(1)} fusion(bf16[128,4096]{1,0:T(8,128)(2,1)} %all-gather.2.cloned.1.call-done, bf16[1024,4096]{1,0:T(8,128)(2,1)} %param.3, f32[128]{0:T(128)S(1)} %add_rsqrt_fusion.1, f32[1024]{0:T(1024)S(1)} %add_rsqrt_fusion), kind=kOutput, calls=%fused_computation.6 | convolution fusion | flops 1074266112 | bytes 9703936 | tf_op jit(solution)/shard_map/dot_general | solution.py:14
  129.4 0.8 copy.4
  (2 shorter events, 0.0 us)
Async XLA Ops:
  6.5 14.4 %copy-start = (bf16[256,4096]{1,0:T(8,128)(2,1)S(1)}, bf16[256,4096]{1,0:T(8,128)(2,1)}, u32[]{:S(2)}) copy-start(bf16[256,4096]{1,0:T(8,128)(2,1)} %param.5) | copy-start | bytes 6291460
  6.5 75.3 %reduce-scatter.2.cloned.1.call-start = ((), (), s32[]{:S(2)}) async-start(), calls=%async_computation.2 | async-start | bytes 2228224 | tf_op jit(solution)/shard_map/reduce_scatter | solution.py:24
  22.8 98.4 %all-gather.2.cloned.1.call-start = ((), (), s32[]{:S(2)}) async-start(), calls=%async_computation.3 | async-start | bytes 1114112 | tf_op jit(solution)/shard_map/all_gather | solution.py:30
Sparse Core Ops, SparseCore 0:
  22.9 58.8 reduce-scatter.1
  84.2 36.9 all-gather.1
where the time goes:
time: 137 us
  waiting for transfers between devices  91.7 us (67%)
  blocking collectives  14.4 us (11%)
  between operations  13.4 us (10%)
  matrix products  8.44 us (6%)
  other arithmetic  8.15 us (6%)
    reduce_scatter x1, waiting for transfers between devices, body(): lax.psum_scatter(jnp.dot(spread, inverse_gram, preferred_element_type=jnp...  59 us
    all_gather x1, waiting for transfers between devices, body(): panel = lax.all_gather(owned, 'row', axis=0, tiled=True)  32.8 us
    all_to_all x1, blocking collectives, body(): lax.all_to_all(query_grads, 'row', split_axis=1, concat_axis=0, tiled=True)  14.4 us
    dot_general x1, matrix products, score_tile(): lax.dot_general(train_grads, panel, (((1,), (1,)), ((), ())), preferred_e...  6.64 us
    reduce_sum x2, other arithmetic, inverse_rms(): return lax.rsqrt(jnp.mean(wide * wide, axis=1) + 1e-06)  6.59 us
  transfers between devices with their start and end apart: 2, of which 2 were waited for; matrix products, arithmetic and copies ran while one was open for 4% of the time, Pallas kernels for 0%

commit v1 on v0

v1 whole, which is shorter than its diff:
```python
import functools

import jax
import jax.numpy as jnp
from jax import lax
from jax.experimental import pallas as pl
from jax.experimental.pallas import tpu as pltpu
from jax.sharding import PartitionSpec as P

CORES = 2
LANES = 128
T_CHUNKS = 8


def flip(value, bits):
    out = value
    bit = 1
    while bit <= bits:
        if bits & bit:
            out = out + bit - 2 * bit * ((out // bit) % 2)
        bit *= 2
    return out


class Gather:
    def __init__(self, dims, slots, recv, send_z, send_y, send_c):
        self.dims = dims
        self.slots, self.recv = slots, recv
        self.send_z, self.send_y, self.send_c = send_z, send_y, send_c
        me = lax.axis_index("row")
        depth, width = dims
        self.c = me % CORES
        self.y = (me // CORES) % width
        self.z = me // (CORES * width)
        self.sends = []

    def row(self, z, y, c):
        return (z * self.dims[1] + y) * CORES + c

    def block(self, dz, dy, dc):
        return self.row(flip(self.z, dz), flip(self.y, dy), flip(self.c, dc))

    def push(self, j, to, sem):
        copy = pltpu.make_async_remote_copy(
            src_ref=self.slots.at[j],
            dst_ref=self.slots.at[j],
            send_sem=sem,
            recv_sem=self.recv.at[j],
            device_id={"row": to},
            device_id_type=pl.DeviceIdType.MESH,
        )
        copy.start()
        self.sends.append(copy)

    def pass_on(self, dz, dy):
        depth, width = self.dims
        j = self.block(dz, dy, 0)
        if dy == 0:
            for k in range(1, width):
                self.push(j, self.block(0, k, 0), self.send_y.at[dz * (width - 1) + k - 1])
        self.push(j, self.block(0, 0, 1), self.send_c.at[dz * width + dy])

    def begin(self):
        depth, width = self.dims
        j = self.block(0, 0, 0)
        for dz in reversed(range(1, depth)):
            self.push(j, self.block(dz, 0, 0), self.send_z.at[dz - 1])
        self.pass_on(0, 0)

    def arrive(self, dz, dy, dc):
        j = self.block(dz, dy, dc)
        slot = self.slots.at[j]
        pltpu.make_async_remote_copy(
            src_ref=slot, dst_ref=slot, send_sem=self.recv.at[j], recv_sem=self.recv.at[j],
            device_id={"row": self.block(0, 0, 1)}, device_id_type=pl.DeviceIdType.MESH,
        ).wait_recv()
        if dc == 0:
            self.pass_on(dz, dy)

    def order(self):
        depth, width = self.dims
        steps = []
        for dz in range(depth):
            if dz:
                steps.append((dz, 0, 0))
            steps.append((dz, 0, 1))
            for dy in range(1, width):
                if dz == 0:
                    continue
                steps.append((dz - 1, dy, 0))
                steps.append((dz - 1, dy, 1))
        for dy in range(1, width):
            steps.append((depth - 1, dy, 0))
            steps.append((depth - 1, dy, 1))
        return steps

    def finish(self):
        for copy in self.sends:
            copy.wait_send()


def kernel(dims, t_hbm, q_ref, g_hbm, out_ref, t_ref, g_ref, q_all, p_all, acc, scale, ssq, t_sem, g_sem,
           q_recv, q_z, q_y, q_c, p_recv, p_z, p_y, p_c):
    depth, width = dims
    n = depth * width * CORES
    rows, proj = t_ref.shape
    blk = g_ref.shape[0]
    nq = out_ref.shape[1]
    tile = rows // T_CHUNKS

    g_copy = pltpu.make_async_copy(g_hbm, g_ref, g_sem)
    g_copy.start()
    t_copies = []
    for i in range(T_CHUNKS):
        span = pl.ds(i * tile, tile)
        t_copies.append(pltpu.make_async_copy(t_hbm.at[span], t_ref.at[span], t_sem.at[i]))
        t_copies[-1].start()

    q_gather = Gather(dims, q_all, q_recv, q_z, q_y, q_c)
    p_gather = Gather(dims, p_all, p_recv, p_z, p_y, p_c)
    me = q_gather.block(0, 0, 0)

    barrier = pltpu.get_barrier_semaphore()
    peers = [q_gather.block(dz, 0, 0) for dz in range(1, depth)]
    peers += [q_gather.block(0, dy, 0) for dy in range(1, width)]
    peers += [q_gather.block(0, 0, 1)]
    for peer in peers:
        pl.semaphore_signal(barrier, inc=1, device_id={"row": peer}, device_id_type=pl.DeviceIdType.MESH)
    q_all[me] = q_ref[...]
    pl.semaphore_wait(barrier, len(peers))

    q_gather.begin()

    def row_scale(i):
        t_copies[i].wait()

        @pl.loop(0, tile // 16)
        def _(s):
            span = pl.ds(pl.multiple_of(i * tile + s * 16, 16), 16)
            total = jnp.zeros((16, LANES), jnp.float32)
            for k in range(proj // LANES):
                wide = t_ref[span, k * LANES:(k + 1) * LANES].astype(jnp.float32)
                total += wide * wide
            mean = jnp.sum(total, axis=1, keepdims=True) * (1.0 / proj)
            scale[span, :] = jnp.broadcast_to(lax.rsqrt(mean + 1e-06), (16, LANES))

    todo = list(range(T_CHUNKS))
    for step in q_gather.order():
        if todo:
            row_scale(todo.pop(0))
        q_gather.arrive(*step)
    for i in todo:
        row_scale(i)
    g_copy.wait()

    queries = q_all[...].astype(jnp.float32).reshape(nq, proj).astype(jnp.bfloat16)
    mine = lax.dot_general(
        g_ref[...], queries, (((1,), (1,)), ((), ())), preferred_element_type=jnp.float32
    ).astype(jnp.bfloat16)
    p_all[me] = mine
    p_gather.begin()

    def add_ssq(j, first=False):
        wide = p_all[j].astype(jnp.float32)
        part = jnp.sum(wide * wide, axis=0, keepdims=True)
        ssq[...] = part if first else ssq[...] + part

    aligned = blk % LANES == 0

    def add(j, first=False):
        add_ssq(j, first)
        if not aligned:
            return
        columns = pl.ds(pl.multiple_of(j * blk, blk), blk)
        part = jnp.dot(t_ref[:, columns], p_all[j], preferred_element_type=jnp.float32)
        acc[...] = part if first else acc[...] + part

    add(me, True)
    for step in p_gather.order():
        p_gather.arrive(*step)
        add(p_gather.block(*step))
    if not aligned:
        panel = p_all[...].reshape(proj, nq)
        acc[...] = jnp.dot(t_ref[...], panel, preferred_element_type=jnp.float32)

    query_scale = lax.rsqrt(ssq[...] * (1.0 / proj) + 1e-06)
    factor = 1.0 / proj ** 0.5
    for k in range(nq // LANES):
        span = slice(k * LANES, (k + 1) * LANES)
        out_ref[:, span] = (acc[:, span] * scale[...] * query_scale[:, span] * factor).astype(out_ref.dtype)
    q_gather.finish()
    p_gather.finish()


def solution(mesh):
    n = mesh.shape["row"]
    width = 2 if mesh.shape["parts"] == 2 else 1
    depth = n // (CORES * width)

    def body(train_grads, query_grads, inverse_gram):
        rows, proj = train_grads.shape
        own = query_grads.shape[0]
        nq = own * n
        blk = inverse_gram.shape[0]
        dma = pltpu.SemaphoreType.DMA
        sems = [
            dma((n,)),
            dma((depth - 1,)),
            dma((max(1, depth * (width - 1)),)),
            dma((depth * width,)),
        ]
        return pl.pallas_call(
            functools.partial(kernel, (depth, width)),
            out_shape=jax.ShapeDtypeStruct((rows, nq), jnp.bfloat16),
            in_specs=[
                pl.BlockSpec(memory_space=pl.ANY),
                pl.BlockSpec(memory_space=pltpu.VMEM),
                pl.BlockSpec(memory_space=pl.ANY),
            ],
            out_specs=pl.BlockSpec(memory_space=pltpu.VMEM),
            scratch_shapes=[
                pltpu.VMEM((rows, proj), jnp.bfloat16),
                pltpu.VMEM((blk, proj), jnp.bfloat16),
                pltpu.VMEM((n, own, proj), jnp.bfloat16),
                pltpu.VMEM((n, blk, nq), jnp.bfloat16),
                pltpu.VMEM((rows, nq), jnp.float32),
                pltpu.VMEM((rows, LANES), jnp.float32),
                pltpu.VMEM((1, nq), jnp.float32),
                dma((T_CHUNKS,)),
                dma,
                *sems,
                *sems,
            ],
            compiler_params=pltpu.CompilerParams(
                collective_id=0, has_side_effects=True, vmem_limit_bytes=56 * 1024 * 1024
            ),
        )(train_grads, query_grads, inverse_gram)

    return jax.shard_map(
        body,
        mesh=mesh,
        in_specs=(P(("parts", "row"), None), P(("parts", "row"), None), P("row", None)),
        out_specs=P(("parts", "row"), None),
        check_vma=False,
    )
```

time: 137 us -> 40.9 us (0.30)
  waiting for transfers between devices: 91.7 us -> 0 us
  Pallas kernels: 0 us -> 38.8 us
  blocking collectives: 14.4 us -> 0 us
  between operations: 13.4 us -> 0.01 us
  matrix products: 8.44 us -> 0 us
  other arithmetic: 8.15 us -> 0 us
    reduce_scatter x1 -> x0, waiting for transfers between devices: 59 us -> none  [body(): lax.psum_scatter(jnp.dot(spread, inverse_gram, preferred_element_type=jnp...]
    pallas_call x0 -> x1, Pallas kernels: none -> 38.8 us  [body(): pl.pallas_call(functools.partial(kernel, (depth, width)), out_shape=jax.S...]
    all_gather x1 -> x0, waiting for transfers between devices: 32.8 us -> none  [body(): panel = lax.all_gather(owned, 'row', axis=0, tiled=True)]
    all_to_all x1 -> x0, blocking collectives: 14.4 us -> none  [body(): lax.all_to_all(query_grads, 'row', split_axis=1, concat_axis=0, tiled=True)]
    dot_general x2 -> x0, matrix products: 8.44 us -> none  [the longest x1 6.64 us: score_tile(): lax.dot_general(train_grads, panel, (((1,), (1,)), ((), ())), preferred_e...]
    reduce_sum x2 -> x0, other arithmetic: 6.59 us -> none  [inverse_rms(): return lax.rsqrt(jnp.mean(wide * wide, axis=1) + 1e-06)]
    unnamed x2 -> x1, local copies, waits for them, and re-layouts: 0.01 us -> 1.67 us
    convert_element_type x1 -> x0, other arithmetic: 1.54 us -> none  [body(): owned = lax.psum_scatter(jnp.dot(spread, inverse_gram, preferred_element_...]
  transfers between devices with their start and end apart: 2 -> 0, of which waited for: 2 -> 0; matrix products, arithmetic and copies ran while one was open for 4% -> 0% of each run, Pallas kernels for 0% -> 0%
where the time goes in v1:
time: 40.9 us; the launch traced here: 40.5 us
  Pallas kernels  38.8 us (95%)
  local copies, waits for them, and re-layouts  1.67 us (4%)
    pallas_call x1, Pallas kernels, body(): pl.pallas_call(functools.partial(kernel, (depth, width)), out_shape=jax.S...  38.8 us
    unnamed x1, local copies, waits for them, and re-layouts  1.67 us

profile of v1, /device:TPU:0, one launch (start us, length us, event | category | flops | bytes accessed | tf_op | source)
XLA Modules:
  0.0 40.5 jit_solution(15240920707447869807)
XLA Ops:
  0.0 38.8 %shard_map.37 = bf16[1024,128]{1,0:T(8,128)(2,1)} custom-call(bf16[1024,4096]{1,0:T(8,128)(2,1)} %t_hbm.1, bf16[8,4096]{1,0:T(8,128)(2,1)} %q_ref.1, bf16[256,4096]{1,0:T(8,128)(2,1)} %g_hbm.1), custom_call_target="tpu_custom_call" | custom-call | tf_op jit(solution)/shard_map/pallas_call | solution.py:212
  38.8 1.7 %copy.5 = bf16[1024,128]{1,0:T(8,128)(2,1)} copy(bf16[1024,128]{1,0:T(8,128)(2,1)} %shard_map.37) | data formatting | bytes 524288

commit v2 on v1

v2 whole, which is shorter than its diff:
```python
import functools

import jax
import jax.numpy as jnp
from jax import lax
from jax.experimental import pallas as pl
from jax.experimental.pallas import tpu as pltpu
from jax.sharding import PartitionSpec as P

CORES = 2
LANES = 128
T_CHUNKS = 8
Q_PIECES = 1
P_PIECES = 1


def flip(value, bits):
    out = value
    bit = 1
    while bit <= bits:
        if bits & bit:
            out = out + bit - 2 * bit * ((out // bit) % 2)
        bit *= 2
    return out


class Gather:
    def __init__(self, dims, slots, recv, sent):
        self.dims = dims
        self.slots, self.recv, self.sent = slots, recv, sent
        me = lax.axis_index("row")
        depth, width = dims
        self.c = me % CORES
        self.y = (me // CORES) % width
        self.z = me // (CORES * width)
        self.sends = []

    def block(self, dz, dy, dc):
        z, y, c = flip(self.z, dz), flip(self.y, dy), flip(self.c, dc)
        return (z * self.dims[1] + y) * CORES + c

    def push(self, j, piece, to):
        slot = self.slots.at[j, piece]
        copy = pltpu.make_async_remote_copy(
            src_ref=slot,
            dst_ref=slot,
            send_sem=self.sent.at[len(self.sends)],
            recv_sem=self.recv.at[j, piece],
            device_id={"row": to},
            device_id_type=pl.DeviceIdType.MESH,
        )
        copy.start()
        self.sends.append(copy)

    def step(self, entry):
        block, piece, targets = entry
        j = self.block(*block)
        if block != (0, 0, 0):
            slot = self.slots.at[j, piece]
            pltpu.make_async_remote_copy(
                src_ref=slot,
                dst_ref=slot,
                send_sem=self.recv.at[j, piece],
                recv_sem=self.recv.at[j, piece],
                device_id={"row": self.block(0, 0, 1)},
                device_id_type=pl.DeviceIdType.MESH,
            ).wait_recv()
        for target in targets:
            self.push(j, piece, self.block(*target))

    def finish(self):
        for copy in self.sends:
            copy.wait_send()


def make_plan(dims, pieces):
    depth, width = dims
    across = [(0, dy, 0) for dy in range(1, width)]
    core = [(0, 0, 1)]
    routes = {(dz, 0, 0): across + core for dz in range(1, depth)}
    routes.update({(dz, dy, 0): core for dz in range(depth) for dy in range(1, width)})
    first = [(1, 0, 0)] + across + core + [(dz, 0, 0) for dz in range(2, depth)]
    order = [(1, 0, 0)] + across
    for dz in range(2, depth):
        order += [(dz, 0, 0)] + [(dz - 1, dy, 0) for dy in range(1, width)]
    order += [(depth - 1, dy, 0) for dy in range(1, width)]
    plan = [((0, 0, 0), p, first) for p in range(pieces)]
    plan += [(block, p, routes[block]) for block in order for p in range(pieces)]
    late = [((block[0], block[1], 1), p, []) for block, p, _ in plan]
    return plan, late


def kernel(dims, t_hbm, q_ref, g_hbm, out_ref, t_ref, g_ref, q_all, p_all, acc, squares, ssq, t_sem, g_sem,
           q_recv, q_sent, p_recv, p_sent):
    depth, width = dims
    rows, proj = t_ref.shape
    blk = g_ref.shape[0]
    own, nq = q_ref.shape[0], out_ref.shape[1]
    tile = rows // T_CHUNKS

    g_copy = pltpu.make_async_copy(g_hbm, g_ref, g_sem)
    g_copy.start()
    t_copies = []
    for i in range(T_CHUNKS):
        span = pl.ds(i * tile, tile)
        t_copies.append(pltpu.make_async_copy(t_hbm.at[span], t_ref.at[span], t_sem.at[i]))
        t_copies[-1].start()

    q_gather = Gather(dims, q_all, q_recv, q_sent)
    p_gather = Gather(dims, p_all, p_recv, p_sent)
    me = q_gather.block(0, 0, 0)

    barrier = pltpu.get_barrier_semaphore()
    peers = []
    for _, _, targets in make_plan(dims, 1)[0]:
        peers += [target for target in targets if target not in peers]
    peers = [q_gather.block(*peer) for peer in peers]
    for peer in peers:
        pl.semaphore_signal(barrier, inc=1, device_id={"row": peer}, device_id_type=pl.DeviceIdType.MESH)
    cut = proj // Q_PIECES
    for p in range(Q_PIECES):
        q_all[me, p] = q_ref[:, p * cut:(p + 1) * cut]
    pl.semaphore_wait(barrier, len(peers))

    def row_squares(i):
        t_copies[i].wait()

        @pl.loop(0, tile // 32)
        def _(s):
            span = pl.ds(pl.multiple_of(i * tile + s * 32, 32), 32)
            total = jnp.zeros((32, LANES), jnp.float32)
            for k in range(proj // LANES):
                wide = t_ref[span, k * LANES:(k + 1) * LANES].astype(jnp.float32)
                total += wide * wide
            squares[span, :] = total

    todo = list(range(T_CHUNKS))
    plan, late = make_plan(dims, Q_PIECES)
    for entry in plan:
        q_gather.step(entry)
        if todo and entry[1] == Q_PIECES - 1:
            row_squares(todo.pop(0))
    for entry in late:
        q_gather.step(entry)
    for i in todo:
        row_squares(i)
    g_copy.wait()

    mine = None
    for p in range(Q_PIECES):
        queries = q_all[:, p].astype(jnp.float32).reshape(nq, cut).astype(jnp.bfloat16)
        part = lax.dot_general(
            g_ref[:, p * cut:(p + 1) * cut], queries, (((1,), (1,)), ((), ())),
            preferred_element_type=jnp.float32,
        )
        mine = part if mine is None else mine + part
    panel = mine.astype(jnp.bfloat16)
    high = blk // P_PIECES
    for p in range(P_PIECES):
        p_all[me, p] = panel[p * high:(p + 1) * high]

    aligned = blk % LANES == 0

    def add(j, first=False):
        block = p_all[j].reshape(blk, nq)
        wide = block.astype(jnp.float32)
        part = jnp.sum(wide * wide, axis=0, keepdims=True)
        ssq[...] = part if first else ssq[...] + part
        if not aligned:
            return
        columns = pl.ds(pl.multiple_of(j * blk, blk), blk)
        part = jnp.dot(t_ref[:, columns], block, preferred_element_type=jnp.float32)
        acc[...] = part if first else acc[...] + part

    plan, late = make_plan(dims, P_PIECES)
    done = []
    for entry in plan:
        p_gather.step(entry)
        if entry[1] == P_PIECES - 1:
            add(p_gather.block(*entry[0]), not done)
            done.append(entry[0])
            if len(done) > 2:
                for other in late:
                    if other[0][:2] == done[-3][:2]:
                        p_gather.step(other)
                add(p_gather.block(*done[-3][:2], 1))
    for block in done[-2:]:
        for other in late:
            if other[0][:2] == block[:2]:
                p_gather.step(other)
        add(p_gather.block(*block[:2], 1))
    if not aligned:
        whole = p_all[...].reshape(proj, nq)
        acc[...] = jnp.dot(t_ref[...], whole, preferred_element_type=jnp.float32)

    scale = lax.rsqrt(jnp.sum(squares[...], axis=1, keepdims=True) * (1.0 / proj) + 1e-06)
    query_scale = lax.rsqrt(ssq[...] * (1.0 / proj) + 1e-06)
    factor = 1.0 / proj ** 0.5
    out_ref[...] = (acc[...] * scale * query_scale * factor).astype(out_ref.dtype)
    q_gather.finish()
    p_gather.finish()


def solution(mesh):
    n = mesh.shape["row"]
    width = 2 if mesh.shape["parts"] == 2 else 1
    depth = n // (CORES * width)

    def body(train_grads, query_grads, inverse_gram):
        rows, proj = train_grads.shape
        own = query_grads.shape[0]
        nq = own * n
        blk = inverse_gram.shape[0]
        dma = pltpu.SemaphoreType.DMA

        def sems(pieces):
            plan, late = make_plan((depth, width), pieces)
            return [dma((n, pieces)), dma((sum(len(entry[2]) for entry in plan),))]

        return pl.pallas_call(
            functools.partial(kernel, (depth, width)),
            out_shape=jax.ShapeDtypeStruct((rows, nq), jnp.bfloat16),
            in_specs=[
                pl.BlockSpec(memory_space=pl.ANY),
                pl.BlockSpec(memory_space=pltpu.VMEM),
                pl.BlockSpec(memory_space=pl.ANY),
            ],
            out_specs=pl.BlockSpec(memory_space=pltpu.VMEM),
            scratch_shapes=[
                pltpu.VMEM((rows, proj), jnp.bfloat16),
                pltpu.VMEM((blk, proj), jnp.bfloat16),
                pltpu.VMEM((n, Q_PIECES, own, proj // Q_PIECES), jnp.bfloat16),
                pltpu.VMEM((n, P_PIECES, blk // P_PIECES, nq), jnp.bfloat16),
                pltpu.VMEM((rows, nq), jnp.float32),
                pltpu.VMEM((rows, LANES), jnp.float32),
                pltpu.VMEM((1, nq), jnp.float32),
                dma((T_CHUNKS,)),
                dma,
                *sems(Q_PIECES),
                *sems(P_PIECES),
            ],
            compiler_params=pltpu.CompilerParams(
                collective_id=0, has_side_effects=True, vmem_limit_bytes=56 * 1024 * 1024
            ),
        )(train_grads, query_grads, inverse_gram)

    return jax.shard_map(
        body,
        mesh=mesh,
        in_specs=(P(("parts", "row"), None), P(("parts", "row"), None), P("row", None)),
        out_specs=P(("parts", "row"), None),
        check_vma=False,
    )
```

time: 40.9 us -> 35 us (0.86)
  Pallas kernels: 38.8 us -> 33.2 us
    pallas_call x1, Pallas kernels: 38.8 us -> 33.2 us  [body(): pl.pallas_call(functools.partial(kernel, (depth, width)), out_shape=jax.S...]
where the time goes in v2:
time: 35 us; the launch traced here: 34.8 us
  Pallas kernels  33.2 us (95%)
  local copies, waits for them, and re-layouts  1.67 us (5%)
    pallas_call x1, Pallas kernels, body(): pl.pallas_call(functools.partial(kernel, (depth, width)), out_shape=jax.S...  33.2 us
    unnamed x1, local copies, waits for them, and re-layouts  1.67 us

profile of v2, /device:TPU:0, one launch (start us, length us, event | category | flops | bytes accessed | tf_op | source)
XLA Modules:
  0.0 34.8 jit_solution(7828594678679102612)
XLA Ops:
  0.0 33.2 %shard_map.37 = bf16[1024,128]{1,0:T(8,128)(2,1)} custom-call(bf16[1024,4096]{1,0:T(8,128)(2,1)} %t_hbm.1, bf16[8,4096]{1,0:T(8,128)(2,1)} %q_ref.1, bf16[256,4096]{1,0:T(8,128)(2,1)} %g_hbm.1), custom_call_target="tpu_custom_call" | custom-call | tf_op jit(solution)/shard_map/pallas_call | solution.py:220
  33.2 1.7 %copy.5 = bf16[1024,128]{1,0:T(8,128)(2,1)} copy(bf16[1024,128]{1,0:T(8,128)(2,1)} %shard_map.37) | data formatting | bytes 524288

commit v3 on v2

--- a/solution.py
+++ b/solution.py
@@ -9,7 +9,7 @@
 
 CORES = 2
 LANES = 128
-T_CHUNKS = 8
+T_CHUNKS = 16
 Q_PIECES = 1
 P_PIECES = 1
 
@@ -141,6 +141,8 @@
         if todo and entry[1] == Q_PIECES - 1:
             row_squares(todo.pop(0))
     for entry in late:
+        if todo:
+            row_squares(todo.pop(0))
         q_gather.step(entry)
     for i in todo:
         row_squares(i)
@@ -172,12 +174,21 @@
         part = jnp.dot(t_ref[:, columns], block, preferred_element_type=jnp.float32)
         acc[...] = part if first else acc[...] + part
 
+    factor = 1.0 / proj ** 0.5
+
+    def row_scale():
+        total = jnp.sum(squares[...], axis=1, keepdims=True)
+        scale = lax.rsqrt(total * (1.0 / proj) + 1e-06) * factor
+        squares[...] = jnp.broadcast_to(scale, squares.shape)
+
     plan, late = make_plan(dims, P_PIECES)
     done = []
     for entry in plan:
         p_gather.step(entry)
         if entry[1] == P_PIECES - 1:
             add(p_gather.block(*entry[0]), not done)
+            if not done:
+                row_scale()
             done.append(entry[0])
             if len(done) > 2:
                 for other in late:
@@ -193,10 +204,10 @@
         whole = p_all[...].reshape(proj, nq)
         acc[...] = jnp.dot(t_ref[...], whole, preferred_element_type=jnp.float32)
 
-    scale = lax.rsqrt(jnp.sum(squares[...], axis=1, keepdims=True) * (1.0 / proj) + 1e-06)
     query_scale = lax.rsqrt(ssq[...] * (1.0 / proj) + 1e-06)
-    factor = 1.0 / proj ** 0.5
-    out_ref[...] = (acc[...] * scale * query_scale * factor).astype(out_ref.dtype)
+    for k in range(nq // LANES):
+        span = slice(k * LANES, (k + 1) * LANES)
+        out_ref[:, span] = (acc[:, span] * squares[...] * query_scale[:, span]).astype(out_ref.dtype)
     q_gather.finish()
     p_gather.finish()
 

time: 35 us -> 35.6 us (1.017)
  Pallas kernels: 33.2 us -> 33.8 us
    pallas_call x1, Pallas kernels: 33.2 us -> 33.8 us  [body(): pl.pallas_call(functools.partial(kernel, (depth, width)), out_shape=jax.S...]
where the time goes in v3:
time: 35.6 us; the launch traced here: 35.4 us
  Pallas kernels  33.8 us (95%)
  local copies, waits for them, and re-layouts  1.67 us (5%)
    pallas_call x1, Pallas kernels, body(): pl.pallas_call(functools.partial(kernel, (depth, width)), out_shape=jax.S...  33.8 us
    unnamed x1, local copies, waits for them, and re-layouts  1.67 us

profile of v3, /device:TPU:0, one launch (start us, length us, event | category | flops | bytes accessed | tf_op | source)
XLA Modules:
  0.0 35.4 jit_solution(6097110642435960320)
XLA Ops:
  0.0 33.8 %shard_map.37 = bf16[1024,128]{1,0:T(8,128)(2,1)} custom-call(bf16[1024,4096]{1,0:T(8,128)(2,1)} %t_hbm.1, bf16[8,4096]{1,0:T(8,128)(2,1)} %q_ref.1, bf16[256,4096]{1,0:T(8,128)(2,1)} %g_hbm.1), custom_call_target="tpu_custom_call" | custom-call | tf_op jit(solution)/shard_map/pallas_call | solution.py:231
  33.8 1.7 %copy.5 = bf16[1024,128]{1,0:T(8,128)(2,1)} copy(bf16[1024,128]{1,0:T(8,128)(2,1)} %shard_map.37) | data formatting | bytes 524288
